TPU v7x, 32 devices: a whole 2x2x4 slice. The times are simulated.
32 devices in a mesh: sec: 2 (over core), tile: 16 (over z, y, x).
Axes of the slice: x: 2, y: 2, z: 4, core: 2. Of those that a mesh axis runs over, the one named last changes fastest.
Arguments:
- displacement: float32 [2, 2, 32, 4096], P('sec', None, 'tile'), may hold values from -6 to 6
- stiffness: float32 [2, 32, 4096], P('sec', 'tile'), may hold values from 0.5 to 2
- match_weight: float32 [2, 48, 512], P('sec', 'tile'), may hold values from 0.5 to 4
- match_offset: float32 [2, 2, 48, 512], P('sec', None, 'tile'), may hold values from -6 to 6
- source_row: int32 [2, 48, 512], P('sec', 'tile'), may hold values from 0 to 1
- source_col: int32 [2, 48, 512], P('sec', 'tile'), may hold values from 0 to 4095
- target_row: int32 [2, 48, 512], P('sec', 'tile'), may hold values from 0 to 1
- target_col: int32 [2, 48, 512], P('sec', 'tile'), may hold values from 0 to 4095
- match_count: int32 [2, 48], P('sec', 'tile'), may hold values from 0 to 512, as said below
Outputs:
- aligned: float32 [2, 2, 32, 4096], P('sec', None, 'tile')
Inputs may be any that keep to these rules, and one draw needn't show every extreme that they name: `match_count`: in every section some tile's group 1 uses all 512 slots, and some tile other than the first and the last uses all 512 slots in group 0 and in group 2.
All inputs are finite; a program needn't handle non-finite values.
Results may differ from a plain program's by a relative error of at most 0.0018.
Values sent between devices are 32-bit elements; how exact they have to be, the bound alone decides.
A program may use at most 64 MiB of HBM per device.

v0:
```python
import functools
import jax
import jax.numpy as jnp
from jax import lax
from jax.experimental import pallas as pl
from jax.experimental.pallas import tpu as pltpu
from jax.sharding import PartitionSpec as P

STEPS = 2
DAMPING = 0.7
LANES = 128
MESH = pl.DeviceIdType.MESH


def stencil(rows, above, below):
    chunks = rows[0].shape[0]
    lane = lax.broadcasted_iota(jnp.int32, rows[0].shape, 1)
    chunk = lax.broadcasted_iota(jnp.int32, rows[0].shape, 0)
    sums = []
    for here, beside in ((rows[0], above + rows[1]), (rows[1], rows[0] + below)):
        both = here + 0.5 * beside
        left = pltpu.roll(both, 1, 1)
        left = jnp.where(lane == 0, jnp.where(chunk == 0, 0.0, pltpu.roll(left, 1, 0)), left)
        right = pltpu.roll(both, LANES - 1, 1)
        right = jnp.where(
            lane == LANES - 1,
            jnp.where(chunk == chunks - 1, 0.0, pltpu.roll(right, chunks - 1, 0)),
            right,
        )
        sums.append(beside + left + right)
    return sums


def two_parts(values):
    high = values.astype(jnp.bfloat16)
    low = (values - high.astype(jnp.float32)).astype(jnp.bfloat16)
    return high, low


def kernel(
    n_sec, n_tile, disp_in, stiff_in, wgt_in, off_in, srow_in, scol_in, trow_in, tcol_in, cnt_in,
    out,
    disp, stiff, wgt, off, rows, cols, cnt, load_sem,
    field, force, total, inv, lhs, hot_lo, hot_hi, hi_ids, edge, halo, mine, theirs, weights,
    edge_send, edge_recv, val_send, val_recv, wgt_send, wgt_recv,
):
    sec = lax.axis_index("sec")
    tile = lax.axis_index("tile")
    chunks = field.shape[2]
    nodes_hi = 2 * chunks
    slots = wgt.shape[2]
    has_tile = [tile > 0, None, tile < n_tile - 1]
    first_role = jnp.where(sec < n_sec - 1, 0, 1)
    end_role = jnp.where(sec > 0, 2, 1)
    sides = ((0, 0), (2, 1))

    def when_tile(g, body):
        if has_tile[g] is None:
            body()
        else:
            pl.when(has_tile[g])(body)

    def each_role(body):
        def turn(role, carry):
            body(role)
            return carry

        lax.fori_loop(first_role, end_role, turn, jnp.int32(0))

    barrier = pltpu.get_barrier_semaphore()

    def greet(s, t):
        pl.semaphore_signal(barrier, inc=1, device_id=(s, t), device_id_type=MESH)

    for g in (0, 2):
        when_tile(g, lambda g=g: greet(sec, tile + g - 1))
    def greet_role(role):
        for g in (0, 2, 1):
            when_tile(g, lambda g=g: greet(sec + 1 - 2 * role, tile + g - 1))

    each_role(greet_role)

    low_side = jnp.where(tile > 0, 1, 0)
    high_side = jnp.where(tile < n_tile - 1, 1, 0)
    secs = jnp.where(sec > 0, 1, 0) + jnp.where(sec < n_sec - 1, 1, 0)
    greetings = low_side + high_side + secs * (1 + low_side + high_side)

    loads = [
        pltpu.make_async_copy(source, target, load_sem.at[i])
        for i, (source, target) in enumerate(
            (
                (disp_in, disp),
                (stiff_in, stiff),
                (scol_in, cols.at[0]),
                (srow_in, rows.at[0]),
                (tcol_in, cols.at[1]),
                (trow_in, rows.at[1]),
                (off_in, off.at[0]),
                (wgt_in, wgt),
                (cnt_in, cnt),
            )
        )
    ]
    for load in loads:
        load.start()

    def edge_copy(step, side, k, landed=False):
        to_side = side if landed else 1 - side
        return pltpu.make_async_remote_copy(
            src_ref=edge.at[step, side, k],
            dst_ref=halo.at[step, to_side, k],
            send_sem=edge_send.at[step, side, k],
            recv_sem=edge_recv.at[step, to_side, k],
            device_id=(sec, tile + 2 * side - 1),
            device_id_type=MESH,
        )

    def value_copy(step, role, g, landed=False):
        to_role, to_g = (role, g) if landed else (1 - role, 2 - g)
        return pltpu.make_async_remote_copy(
            src_ref=mine.at[step, role, g],
            dst_ref=theirs.at[step, to_role, to_g],
            send_sem=val_send.at[step, role, g],
            recv_sem=val_recv.at[step, to_role, to_g],
            device_id=(sec + 1 - 2 * role, tile + g - 1),
            device_id_type=MESH,
        )

    def weight_copy(g, landed=False):
        role = 1 if landed else 0
        to_g = g if landed else 2 - g
        return pltpu.make_async_remote_copy(
            src_ref=weights.at[0, g],
            dst_ref=weights.at[1, to_g],
            send_sem=wgt_send.at[g],
            recv_sem=wgt_recv.at[to_g],
            device_id=(sec + 1 - 2 * role, tile + g - 1),
            device_id_type=MESH,
        )

    def send_edges(step, k):
        for g, side in sides:
            pl.when(has_tile[g])(lambda side=side: edge_copy(step, side, k).start())

    def await_edges(step, k):
        for g, side in sides:
            pl.when(has_tile[g])(lambda side=side: edge_copy(step, side, k, True).wait_recv())

    for g, side in sides:

        @pl.when(jnp.logical_not(has_tile[g]))
        def _(g=g, side=side):
            halo[:, side] = jnp.zeros((STEPS,) + halo.shape[2:], jnp.float32)
            for role in range(2):
                weights[role, g] = jnp.zeros(weights.shape[2:], jnp.float32)
                for step in range(STEPS):
                    theirs[step, role, g] = jnp.zeros(theirs.shape[3:], jnp.float32)

    lane_slot = lax.broadcasted_iota(jnp.int32, (1, slots), 1)
    lo_node = lax.broadcasted_iota(jnp.int32, (LANES, slots), 0)
    hi_node = lax.broadcasted_iota(jnp.int32, (nodes_hi, slots), 0)

    loads[0].wait()
    loads[1].wait()
    for r in range(2):
        c_row = stiff[pl.ds(r, chunks, stride=2), :]
        edge[0, r, 2] = c_row
        for k in range(2):
            u_row = disp[k, pl.ds(r, chunks, stride=2), :]
            field[k, r] = u_row
            edge[0, r, k] = c_row * u_row

    for load in loads[2:]:
        load.wait()

    off[1] = jnp.zeros(off.shape[1:], jnp.float32)

    @pl.when(sec < n_sec - 1)
    def _():
        for g in range(3):

            def mask(g=g):
                weights[0, g] = jnp.where(lane_slot < cnt[:, g : g + 1], wgt[g], 0.0)

            when_tile(g, mask)

    def prepare(role):
        for g in range(3):
            col = cols[role, g]
            hi = rows[role, g] * chunks + (col >> 7)
            hi_ids[role, g] = hi
            at = pl.ds(g * slots, slots)
            hot = jnp.where(lo_node == (col & (LANES - 1)), 1.0, 0.0).astype(jnp.bfloat16)
            hot_lo[role, pl.ds(0, LANES), at] = hot
            hot_lo[role, pl.ds(LANES, LANES), at] = hot
            hot_hi[role, :, at] = jnp.where(hi_node == hi, 1.0, 0.0).astype(jnp.bfloat16)

    each_role(prepare)

    def pick(step, role):
        for g in (0, 2, 1):
            found = jnp.dot(
                lhs[...],
                hot_lo[role, :, pl.ds(g * slots, slots)],
                preferred_element_type=jnp.float32,
            )
            hit = hi_node == hi_ids[role, g]
            for k in range(2):
                value = jnp.sum(
                    jnp.where(hit, found[k * nodes_hi : (k + 1) * nodes_hi], 0.0),
                    axis=0,
                    keepdims=True,
                )
                mine[step, role, g, pl.ds(k, 1), :] = value - off[role, g, pl.ds(k, 1), :]
        for g in (0, 2, 1):
            when_tile(g, lambda g=g: value_copy(step, role, g).start())

    def spread(role, g, values):
        at = pl.ds(g * slots, slots)
        high = [row.astype(jnp.bfloat16) for row in values]
        low = [(row - h.astype(jnp.float32)).astype(jnp.bfloat16) for row, h in zip(values, high)]
        summed = lax.dot_general(
            jnp.concatenate([hot_hi[role, :, at] * part for part in high + low], axis=0),
            hot_lo[role, pl.ds(0, LANES), at],
            (((1,), (1,)), ((), ())),
            preferred_element_type=jnp.float32,
        )
        half = len(values) * nodes_hi
        return summed[:half] + summed[half:]

    for step in range(STEPS):
        for k in range(2):
            part = two_parts(field[k].reshape(nodes_hi, LANES))
            lhs[pl.ds(k * nodes_hi, nodes_hi), pl.ds(0, LANES)] = part[0]
            lhs[pl.ds(k * nodes_hi, nodes_hi), pl.ds(LANES, LANES)] = part[1]
        if step == 0:
            pl.semaphore_wait(barrier, greetings)
            send_edges(0, 0)

            @pl.when(sec < n_sec - 1)
            def _():
                for g in (0, 2, 1):
                    when_tile(g, lambda g=g: weight_copy(g).start())

        each_role(functools.partial(pick, step))

        if step == 0:
            send_edges(0, 2)
        send_edges(step, 1)

        if step == 0:
            inv[...] = jnp.zeros(inv.shape, jnp.float32)

            def spread_weights(role):
                @pl.when(role == 1)
                def _():
                    for g in range(3):
                        when_tile(g, lambda g=g: weight_copy(g, True).wait_recv())

                at = sum(spread(role, g, [weights[role, g]]) for g in range(3))
                inv[...] += at.reshape(inv.shape)

            each_role(spread_weights)

        force[...] = jnp.zeros(force.shape, jnp.float32)

        def spread_pulls(role, step=step):
            for batch in ((1,), (0, 2)):
                for g in batch:
                    when_tile(g, lambda g=g: value_copy(step, role, g, True).wait_recv())
                at = 0.0
                for g in batch:
                    pull = weights[role, g] * (theirs[step, role, g] - mine[step, role, g])
                    at = at + spread(role, g, [pull[0:1], pull[1:2]])
                force[...] += at.reshape(force.shape)

        each_role(spread_pulls)

        if step == 0:
            await_edges(0, 2)
            c_rows = [edge[0, r, 2] for r in range(2)]
            sums = stencil(c_rows, halo[0, 0, 2], halo[0, 1, 2])
            for r in range(2):
                springs = c_rows[r] * sums[r]
                total[r] = springs
                inv[r] = DAMPING / (inv[r] + springs)

        for k in range(2):
            await_edges(step, k)
            sums = stencil([edge[step, r, k] for r in range(2)], halo[step, 0, k], halo[step, 1, k])
            for r in range(2):
                c_row = edge[0, r, 2]
                here = field[k, r]
                pulled = force[k, r] + c_row * sums[r] - here * total[r]
                new = here + pulled * inv[r]
                if step < STEPS - 1:
                    field[k, r] = new
                    edge[step + 1, r, k] = c_row * new
                else:
                    out[k, pl.ds(r, chunks, stride=2), :] = new
            if step < STEPS - 1 and k == 0:
                send_edges(step + 1, 0)

    for step in range(STEPS):
        for k in range(3 if step == 0 else 2):
            for g, side in sides:
                pl.when(has_tile[g])(
                    lambda side=side: edge_copy(step, side, k).wait_send()
                )

        def drain(role, step=step):
            for g in range(3):
                when_tile(g, lambda g=g: value_copy(step, role, g).wait_send())

        each_role(drain)

    @pl.when(sec < n_sec - 1)
    def _():
        for g in range(3):
            when_tile(g, lambda g=g: weight_copy(g).wait_send())


def relax(n_sec, n_tile, *args):
    displacement, stiffness, weight, offset, srow, scol, trow, tcol, count = args
    rows, width = stiffness.shape[1:]
    slots = weight.shape[2]
    chunks = width // LANES
    nodes_hi = rows * chunks

    def interleaved(x):
        x = x.reshape(-1, rows, chunks, LANES).transpose(0, 2, 1, 3)
        return x.reshape(-1, nodes_hi, LANES)

    operands = (
        interleaved(displacement), interleaved(stiffness)[0], weight.transpose(1, 0, 2),
        offset[0].transpose(1, 0, 2), srow.transpose(1, 0, 2), scol.transpose(1, 0, 2),
        trow.transpose(1, 0, 2), tcol.transpose(1, 0, 2), count,
    )
    vmem = pl.BlockSpec(memory_space=pltpu.VMEM)
    dma = pltpu.SemaphoreType.DMA
    f32 = jnp.float32
    out = pl.pallas_call(
        functools.partial(kernel, n_sec, n_tile),
        out_shape=jax.ShapeDtypeStruct((2, nodes_hi, LANES), f32),
        in_specs=[pl.BlockSpec(memory_space=pltpu.HBM)] * 9,
        out_specs=vmem,
        scratch_shapes=[
            pltpu.VMEM((2, nodes_hi, LANES), f32),
            pltpu.VMEM((nodes_hi, LANES), f32),
            pltpu.VMEM((3, 1, slots), f32),
            pltpu.VMEM((2, 3, 2, slots), f32),
            pltpu.VMEM((2, 3, 1, slots), jnp.int32),
            pltpu.VMEM((2, 3, 1, slots), jnp.int32),
            pltpu.VMEM((1, 3), jnp.int32),
            dma((9,)),
            pltpu.VMEM((2, rows, chunks, LANES), f32),
            pltpu.VMEM((2, rows, chunks, LANES), f32),
            pltpu.VMEM((rows, chunks, LANES), f32),
            pltpu.VMEM((rows, chunks, LANES), f32),
            pltpu.VMEM((2 * nodes_hi, 2 * LANES), jnp.bfloat16),
            pltpu.VMEM((2, 2 * LANES, 3 * slots), jnp.bfloat16),
            pltpu.VMEM((2, nodes_hi, 3 * slots), jnp.bfloat16),
            pltpu.VMEM((2, 3, 1, slots), jnp.int32),
            pltpu.VMEM((STEPS, 2, 3, chunks, LANES), f32),
            pltpu.VMEM((STEPS, 2, 3, chunks, LANES), f32),
            pltpu.VMEM((STEPS, 2, 3, 2, slots), f32),
            pltpu.VMEM((STEPS, 2, 3, 2, slots), f32),
            pltpu.VMEM((2, 3, 1, slots), f32),
            dma((STEPS, 2, 3)),
            dma((STEPS, 2, 3)),
            dma((STEPS, 2, 3)),
            dma((STEPS, 2, 3)),
            dma((3,)),
            dma((3,)),
        ],
        compiler_params=pltpu.CompilerParams(
            collective_id=0, has_side_effects=True, vmem_limit_bytes=24 * 1024 * 1024
        ),
    )(*[pltpu.with_memory_space_constraint(x, pltpu.HBM) for x in operands])
    out = out.reshape(2, chunks, rows, LANES).transpose(0, 2, 1, 3)
    return out.reshape(1, 2, rows, width)


def solution(mesh):
    placed = (
        P("sec", None, "tile", None),
        P("sec", "tile", None),
        P("sec", "tile", None),
        P("sec", None, "tile", None),
        P("sec", "tile", None),
        P("sec", "tile", None),
        P("sec", "tile", None),
        P("sec", "tile", None),
        P("sec", "tile"),
    )
    return jax.shard_map(
        functools.partial(relax, mesh.shape["sec"], mesh.shape["tile"]),
        mesh=mesh, in_specs=placed, out_specs=P("sec", None, "tile", None), check_vma=False,
    )
```

profile of v0, /device:TPU:0, one launch (start us, length us, event | category | flops | bytes accessed | tf_op | source)
XLA Modules:
  0.0 12.6 jit_solution(6468120606320117295)
XLA Ops:
  0.0 12.0 %shard_map.91 = f32[2,64,128]{2,1,0:T(8,128)S(1)} custom-call(f32[2,64,128]{2,1,0:T(8,128)} %bitcast.24, f32[64,128]{1,0:T(8,128)} %bitcast.25, f32[3,1,512]{2,1,0:T(1,128)} %bitcast.27, f32[3,2,512]{2,1,0:T(2,128)} %bitcast.26, s32[3,1,512]{2,1,0:T(1,128)} %bitcast.28, s32[3,1,512]{2,1,0:T(1,128)} %bitcast.29, s32[3,1,512]{2,1,0:T(1,128)} %bitcast.30, ...), custom_call_target="tpu_custom_call" | custom-call | tf_op jit(solution)/shard_map/pallas_call | solution.py:342
  12.0 0.6 %copy.14 = f32[1,2,2,4096]{3,2,1,0:T(2,128)} copy(f32[1,2,2,4096]{3,2,1,0:T(2,128)S(1)} %bitcast.23) | data formatting | bytes 131072
where the time goes:
time: 12.8 us; the launch traced here: 12.6 us
  Pallas kernels  12 us (94%)
  local copies, waits for them, and re-layouts  0.63 us (5%)
    pallas_call x1, Pallas kernels, relax(): pl.pallas_call(functools.partial(kernel, n_sec, n_tile), out_shape=jax.Sh...  12 us
    unnamed x1, local copies, waits for them, and re-layouts  0.63 us

commit v1 on v0

--- a/solution.py
+++ b/solution.py
@@ -170,6 +170,9 @@
             field[k, r] = u_row
             edge[0, r, k] = c_row * u_row
 
+    pl.semaphore_wait(barrier, greetings)
+    send_edges(0, 0)
+    send_edges(0, 2)
     for load in loads[2:]:
         load.wait()
 
@@ -228,14 +231,32 @@
         half = len(values) * nodes_hi
         return summed[:half] + summed[half:]
 
+    def drain(step):
+        def drain_role(role):
+            for g in range(3):
+                when_tile(g, lambda g=g: value_copy(step, role, g).wait_send())
+
+        each_role(drain_role)
+        if step == 0:
+
+            @pl.when(sec < n_sec - 1)
+            def _():
+                for g in range(3):
+                    when_tile(g, lambda g=g: weight_copy(g).wait_send())
+
+        for g, side in sides:
+
+            @pl.when(has_tile[g])
+            def _(side=side):
+                for k in range(3 if step == 0 else 2):
+                    edge_copy(step, side, k).wait_send()
+
     for step in range(STEPS):
         for k in range(2):
             part = two_parts(field[k].reshape(nodes_hi, LANES))
             lhs[pl.ds(k * nodes_hi, nodes_hi), pl.ds(0, LANES)] = part[0]
             lhs[pl.ds(k * nodes_hi, nodes_hi), pl.ds(LANES, LANES)] = part[1]
         if step == 0:
-            pl.semaphore_wait(barrier, greetings)
-            send_edges(0, 0)
 
             @pl.when(sec < n_sec - 1)
             def _():
@@ -244,9 +265,9 @@
 
         each_role(functools.partial(pick, step))
 
-        if step == 0:
-            send_edges(0, 2)
         send_edges(step, 1)
+        if step > 0:
+            drain(step - 1)
 
         if step == 0:
             inv[...] = jnp.zeros(inv.shape, jnp.float32)
@@ -301,23 +322,7 @@
             if step < STEPS - 1 and k == 0:
                 send_edges(step + 1, 0)
 
-    for step in range(STEPS):
-        for k in range(3 if step == 0 else 2):
-            for g, side in sides:
-                pl.when(has_tile[g])(
-                    lambda side=side: edge_copy(step, side, k).wait_send()
-                )
-
-        def drain(role, step=step):
-            for g in range(3):
-                when_tile(g, lambda g=g: value_copy(step, role, g).wait_send())
-
-        each_role(drain)
-
-    @pl.when(sec < n_sec - 1)
-    def _():
-        for g in range(3):
-            when_tile(g, lambda g=g: weight_copy(g).wait_send())
+    drain(STEPS - 1)
 
 
 def relax(n_sec, n_tile, *args):

time: 12.8 us -> 13 us (1.016)
  Pallas kernels: 12 us -> 12.2 us
    pallas_call x1, Pallas kernels: 12 us -> 12.2 us  [relax(): pl.pallas_call(functools.partial(kernel, n_sec, n_tile), out_shape=jax.Sh...]
where the time goes in v1:
time: 13 us; the launch traced here: 12.8 us
  Pallas kernels  12.2 us (94%)
  local copies, waits for them, and re-layouts  0.63 us (5%)
    pallas_call x1, Pallas kernels, relax(): pl.pallas_call(functools.partial(kernel, n_sec, n_tile), out_shape=jax.Sh...  12.2 us
    unnamed x1, local copies, waits for them, and re-layouts  0.63 us

profile of v1, /device:TPU:0, one launch (start us, length us, event | category | flops | bytes accessed | tf_op | source)
XLA Modules:
  0.0 12.8 jit_solution(4626321384228271274)
XLA Ops:
  0.0 12.2 %shard_map.91 = f32[2,64,128]{2,1,0:T(8,128)S(1)} custom-call(f32[2,64,128]{2,1,0:T(8,128)} %bitcast.24, f32[64,128]{1,0:T(8,128)} %bitcast.25, f32[3,1,512]{2,1,0:T(1,128)} %bitcast.27, f32[3,2,512]{2,1,0:T(2,128)} %bitcast.26, s32[3,1,512]{2,1,0:T(1,128)} %bitcast.28, s32[3,1,512]{2,1,0:T(1,128)} %bitcast.29, s32[3,1,512]{2,1,0:T(1,128)} %bitcast.30, ...), custom_call_target="tpu_custom_call" | custom-call | tf_op jit(solution)/shard_map/pallas_call | solution.py:347
  12.2 0.6 %copy.14 = f32[1,2,2,4096]{3,2,1,0:T(2,128)} copy(f32[1,2,2,4096]{3,2,1,0:T(2,128)S(1)} %bitcast.23) | data formatting | bytes 131072

commit v2 on v1

--- a/solution.py
+++ b/solution.py
@@ -170,9 +170,6 @@
             field[k, r] = u_row
             edge[0, r, k] = c_row * u_row
 
-    pl.semaphore_wait(barrier, greetings)
-    send_edges(0, 0)
-    send_edges(0, 2)
     for load in loads[2:]:
         load.wait()
 
@@ -215,6 +212,8 @@
                     keepdims=True,
                 )
                 mine[step, role, g, pl.ds(k, 1), :] = value - off[role, g, pl.ds(k, 1), :]
+
+    def send_values(step, role):
         for g in (0, 2, 1):
             when_tile(g, lambda g=g: value_copy(step, role, g).start())
 
@@ -256,6 +255,10 @@
             part = two_parts(field[k].reshape(nodes_hi, LANES))
             lhs[pl.ds(k * nodes_hi, nodes_hi), pl.ds(0, LANES)] = part[0]
             lhs[pl.ds(k * nodes_hi, nodes_hi), pl.ds(LANES, LANES)] = part[1]
+        each_role(functools.partial(pick, step))
+        if step == 0:
+            pl.semaphore_wait(barrier, greetings)
+        each_role(functools.partial(send_values, step))
         if step == 0:
 
             @pl.when(sec < n_sec - 1)
@@ -263,8 +266,8 @@
                 for g in (0, 2, 1):
                     when_tile(g, lambda g=g: weight_copy(g).start())
 
-        each_role(functools.partial(pick, step))
-
+            send_edges(0, 0)
+            send_edges(0, 2)
         send_edges(step, 1)
         if step > 0:
             drain(step - 1)

time: 13 us -> 12.7 us (0.977)
  Pallas kernels: 12.2 us -> 11.9 us
    pallas_call x1, Pallas kernels: 12.2 us -> 11.9 us  [relax(): pl.pallas_call(functools.partial(kernel, n_sec, n_tile), out_shape=jax.Sh...]
where the time goes in v2:
time: 12.7 us; the launch traced here: 12.6 us
  Pallas kernels  11.9 us (94%)
  local copies, waits for them, and re-layouts  0.63 us (5%)
    pallas_call x1, Pallas kernels, relax(): pl.pallas_call(functools.partial(kernel, n_sec, n_tile), out_shape=jax.Sh...  11.9 us
    unnamed x1, local copies, waits for them, and re-layouts  0.63 us

profile of v2, /device:TPU:0, one launch (start us, length us, event | category | flops | bytes accessed | tf_op | source)
XLA Modules:
  0.0 12.6 jit_solution(6595556991398355988)
XLA Ops:
  0.0 11.9 %shard_map.91 = f32[2,64,128]{2,1,0:T(8,128)S(1)} custom-call(f32[2,64,128]{2,1,0:T(8,128)} %bitcast.24, f32[64,128]{1,0:T(8,128)} %bitcast.25, f32[3,1,512]{2,1,0:T(1,128)} %bitcast.27, f32[3,2,512]{2,1,0:T(2,128)} %bitcast.26, s32[3,1,512]{2,1,0:T(1,128)} %bitcast.28, s32[3,1,512]{2,1,0:T(1,128)} %bitcast.29, s32[3,1,512]{2,1,0:T(1,128)} %bitcast.30, ...), custom_call_target="tpu_custom_call" | custom-call | tf_op jit(solution)/shard_map/pallas_call | solution.py:350
  12.0 0.6 %copy.14 = f32[1,2,2,4096]{3,2,1,0:T(2,128)} copy(f32[1,2,2,4096]{3,2,1,0:T(2,128)S(1)} %bitcast.23) | data formatting | bytes 131072

commit v3 on v2

--- a/solution.py
+++ b/solution.py
@@ -67,21 +67,34 @@
 
         lax.fori_loop(first_role, end_role, turn, jnp.int32(0))
 
+    low_side = jnp.where(tile > 0, 1, 0)
+    high_side = jnp.where(tile < n_tile - 1, 1, 0)
+
+    def each_group(body):
+        def turn(g, carry):
+            body(g)
+            return carry
+
+        lax.fori_loop(1 - low_side, 2 + high_side, turn, jnp.int32(0))
+
+    def each_side(body):
+        def turn(side, carry):
+            body(side)
+            return carry
+
+        lax.fori_loop(1 - low_side, 1 + high_side, turn, jnp.int32(0))
+
     barrier = pltpu.get_barrier_semaphore()
 
     def greet(s, t):
         pl.semaphore_signal(barrier, inc=1, device_id=(s, t), device_id_type=MESH)
 
-    for g in (0, 2):
-        when_tile(g, lambda g=g: greet(sec, tile + g - 1))
+    each_side(lambda side: greet(sec, tile + 2 * side - 1))
     def greet_role(role):
-        for g in (0, 2, 1):
-            when_tile(g, lambda g=g: greet(sec + 1 - 2 * role, tile + g - 1))
+        each_group(lambda g: greet(sec + 1 - 2 * role, tile + g - 1))
 
     each_role(greet_role)
 
-    low_side = jnp.where(tile > 0, 1, 0)
-    high_side = jnp.where(tile < n_tile - 1, 1, 0)
     secs = jnp.where(sec > 0, 1, 0) + jnp.where(sec < n_sec - 1, 1, 0)
     greetings = low_side + high_side + secs * (1 + low_side + high_side)
 
@@ -139,12 +152,10 @@
         )
 
     def send_edges(step, k):
-        for g, side in sides:
-            pl.when(has_tile[g])(lambda side=side: edge_copy(step, side, k).start())
+        each_side(lambda side: edge_copy(step, side, k).start())
 
     def await_edges(step, k):
-        for g, side in sides:
-            pl.when(has_tile[g])(lambda side=side: edge_copy(step, side, k, True).wait_recv())
+        each_side(lambda side: edge_copy(step, side, k, True).wait_recv())
 
     for g, side in sides:
 
@@ -185,15 +196,17 @@
             when_tile(g, mask)
 
     def prepare(role):
-        for g in range(3):
+        def one_group(g, carry):
             col = cols[role, g]
             hi = rows[role, g] * chunks + (col >> 7)
             hi_ids[role, g] = hi
-            at = pl.ds(g * slots, slots)
             hot = jnp.where(lo_node == (col & (LANES - 1)), 1.0, 0.0).astype(jnp.bfloat16)
-            hot_lo[role, pl.ds(0, LANES), at] = hot
-            hot_lo[role, pl.ds(LANES, LANES), at] = hot
-            hot_hi[role, :, at] = jnp.where(hi_node == hi, 1.0, 0.0).astype(jnp.bfloat16)
+            hot_lo[role, g, pl.ds(0, LANES)] = hot
+            hot_lo[role, g, pl.ds(LANES, LANES)] = hot
+            hot_hi[role, g] = jnp.where(hi_node == hi, 1.0, 0.0).astype(jnp.bfloat16)
+            return carry
+
+        lax.fori_loop(0, 3, one_group, jnp.int32(0))
 
     each_role(prepare)
 
@@ -201,7 +214,7 @@
         for g in (0, 2, 1):
             found = jnp.dot(
                 lhs[...],
-                hot_lo[role, :, pl.ds(g * slots, slots)],
+                hot_lo[role, g],
                 preferred_element_type=jnp.float32,
             )
             hit = hi_node == hi_ids[role, g]
@@ -214,16 +227,14 @@
                 mine[step, role, g, pl.ds(k, 1), :] = value - off[role, g, pl.ds(k, 1), :]
 
     def send_values(step, role):
-        for g in (0, 2, 1):
-            when_tile(g, lambda g=g: value_copy(step, role, g).start())
+        each_group(lambda g: value_copy(step, role, g).start())
 
     def spread(role, g, values):
-        at = pl.ds(g * slots, slots)
         high = [row.astype(jnp.bfloat16) for row in values]
         low = [(row - h.astype(jnp.float32)).astype(jnp.bfloat16) for row, h in zip(values, high)]
         summed = lax.dot_general(
-            jnp.concatenate([hot_hi[role, :, at] * part for part in high + low], axis=0),
-            hot_lo[role, pl.ds(0, LANES), at],
+            jnp.concatenate([hot_hi[role, g] * part for part in high + low], axis=0),
+            hot_lo[role, g, pl.ds(0, LANES)],
             (((1,), (1,)), ((), ())),
             preferred_element_type=jnp.float32,
         )
@@ -232,63 +243,59 @@
 
     def drain(step):
         def drain_role(role):
-            for g in range(3):
-                when_tile(g, lambda g=g: value_copy(step, role, g).wait_send())
+            each_group(lambda g: value_copy(step, role, g).wait_send())
+
+        def drain_side(side):
+            for k in range(2):
+                edge_copy(step, side, k).wait_send()
 
         each_role(drain_role)
-        if step == 0:
-
-            @pl.when(sec < n_sec - 1)
-            def _():
-                for g in range(3):
-                    when_tile(g, lambda g=g: weight_copy(g).wait_send())
-
-        for g, side in sides:
-
-            @pl.when(has_tile[g])
-            def _(side=side):
-                for k in range(3 if step == 0 else 2):
-                    edge_copy(step, side, k).wait_send()
-
-    for step in range(STEPS):
+        each_side(drain_side)
+
+    def spread_weights(role):
+        @pl.when(role == 1)
+        def _():
+            each_group(lambda g: weight_copy(g, True).wait_recv())
+
+        at = sum(spread(role, g, [weights[role, g]]) for g in range(3))
+        inv[...] += at.reshape(inv.shape)
+
+    def one_step(step, carry):
         for k in range(2):
             part = two_parts(field[k].reshape(nodes_hi, LANES))
             lhs[pl.ds(k * nodes_hi, nodes_hi), pl.ds(0, LANES)] = part[0]
             lhs[pl.ds(k * nodes_hi, nodes_hi), pl.ds(LANES, LANES)] = part[1]
         each_role(functools.partial(pick, step))
-        if step == 0:
+
+        @pl.when(step == 0)
+        def _():
             pl.semaphore_wait(barrier, greetings)
+
         each_role(functools.partial(send_values, step))
-        if step == 0:
-
+
+        @pl.when(step == 0)
+        def _():
             @pl.when(sec < n_sec - 1)
             def _():
-                for g in (0, 2, 1):
-                    when_tile(g, lambda g=g: weight_copy(g).start())
+                each_group(lambda g: weight_copy(g).start())
 
             send_edges(0, 0)
             send_edges(0, 2)
+
         send_edges(step, 1)
-        if step > 0:
+
+        @pl.when(step == 0)
+        def _():
+            inv[...] = jnp.zeros(inv.shape, jnp.float32)
+            each_role(spread_weights)
+
+        @pl.when(step > 0)
+        def _():
             drain(step - 1)
 
-        if step == 0:
-            inv[...] = jnp.zeros(inv.shape, jnp.float32)
-
-            def spread_weights(role):
-                @pl.when(role == 1)
-                def _():
-                    for g in range(3):
-                        when_tile(g, lambda g=g: weight_copy(g, True).wait_recv())
-
-                at = sum(spread(role, g, [weights[role, g]]) for g in range(3))
-                inv[...] += at.reshape(inv.shape)
-
-            each_role(spread_weights)
-
         force[...] = jnp.zeros(force.shape, jnp.float32)
 
-        def spread_pulls(role, step=step):
+        def spread_pulls(role):
             for batch in ((1,), (0, 2)):
                 for g in batch:
                     when_tile(g, lambda g=g: value_copy(step, role, g, True).wait_recv())
@@ -300,7 +307,8 @@
 
         each_role(spread_pulls)
 
-        if step == 0:
+        @pl.when(step == 0)
+        def _():
             await_edges(0, 2)
             c_rows = [edge[0, r, 2] for r in range(2)]
             sums = stencil(c_rows, halo[0, 0, 2], halo[0, 1, 2])
@@ -317,15 +325,26 @@
                 here = field[k, r]
                 pulled = force[k, r] + c_row * sums[r] - here * total[r]
                 new = here + pulled * inv[r]
-                if step < STEPS - 1:
-                    field[k, r] = new
-                    edge[step + 1, r, k] = c_row * new
-                else:
-                    out[k, pl.ds(r, chunks, stride=2), :] = new
-            if step < STEPS - 1 and k == 0:
-                send_edges(step + 1, 0)
-
+                field[k, r] = new
+                edge[step + 1, r, k] = c_row * new
+            if k == 0:
+
+                @pl.when(step < STEPS - 1)
+                def _():
+                    send_edges(step + 1, 0)
+
+        return carry
+
+    lax.fori_loop(0, STEPS, one_step, jnp.int32(0))
+    for k in range(2):
+        for r in range(2):
+            out[k, pl.ds(r, chunks, stride=2), :] = field[k, r]
     drain(STEPS - 1)
+    each_side(lambda side: edge_copy(0, side, 2).wait_send())
+
+    @pl.when(sec < n_sec - 1)
+    def _():
+        each_group(lambda g: weight_copy(g).wait_send())
 
 
 def relax(n_sec, n_tile, *args):
@@ -366,10 +385,10 @@
             pltpu.VMEM((rows, chunks, LANES), f32),
             pltpu.VMEM((rows, chunks, LANES), f32),
             pltpu.VMEM((2 * nodes_hi, 2 * LANES), jnp.bfloat16),
-            pltpu.VMEM((2, 2 * LANES, 3 * slots), jnp.bfloat16),
-            pltpu.VMEM((2, nodes_hi, 3 * slots), jnp.bfloat16),
+            pltpu.VMEM((2, 3, 2 * LANES, slots), jnp.bfloat16),
+            pltpu.VMEM((2, 3, nodes_hi, slots), jnp.bfloat16),
             pltpu.VMEM((2, 3, 1, slots), jnp.int32),
-            pltpu.VMEM((STEPS, 2, 3, chunks, LANES), f32),
+            pltpu.VMEM((STEPS + 1, 2, 3, chunks, LANES), f32),
             pltpu.VMEM((STEPS, 2, 3, chunks, LANES), f32),
             pltpu.VMEM((STEPS, 2, 3, 2, slots), f32),
             pltpu.VMEM((STEPS, 2, 3, 2, slots), f32),

time: 12.7 us -> 12.8 us (level)
  no operation moved by 1% of the time
where the time goes in v3:
time: 12.8 us; the launch traced here: 12.7 us
  Pallas kernels  12 us (94%)
  local copies, waits for them, and re-layouts  0.63 us (5%)
    pallas_call x1, Pallas kernels, relax(): pl.pallas_call(functools.partial(kernel, n_sec, n_tile), out_shape=jax.Sh...  12 us
    unnamed x1, local copies, waits for them, and re-layouts  0.63 us

profile of v3, /device:TPU:0, one launch (start us, length us, event | category | flops | bytes accessed | tf_op | source)
XLA Modules:
  0.0 12.7 jit_solution(266917589379768057)
XLA Ops:
  0.0 12.0 %shard_map.91 = f32[2,64,128]{2,1,0:T(8,128)S(1)} custom-call(f32[2,64,128]{2,1,0:T(8,128)} %bitcast.24, f32[64,128]{1,0:T(8,128)} %bitcast.25, f32[3,1,512]{2,1,0:T(1,128)} %bitcast.27, f32[3,2,512]{2,1,0:T(2,128)} %bitcast.26, s32[3,1,512]{2,1,0:T(1,128)} %bitcast.28, s32[3,1,512]{2,1,0:T(1,128)} %bitcast.29, s32[3,1,512]{2,1,0:T(1,128)} %bitcast.30, ...), custom_call_target="tpu_custom_call" | custom-call | tf_op jit(solution)/shard_map/pallas_call | solution.py:369
  12.0 0.6 %copy.14 = f32[1,2,2,4096]{3,2,1,0:T(2,128)} copy(f32[1,2,2,4096]{3,2,1,0:T(2,128)S(1)} %bitcast.23) | data formatting | bytes 131072

commit v4 on v2

--- a/solution.py
+++ b/solution.py
@@ -275,28 +275,28 @@
         if step == 0:
             inv[...] = jnp.zeros(inv.shape, jnp.float32)
 
-            def spread_weights(role):
-                @pl.when(role == 1)
-                def _():
-                    for g in range(3):
-                        when_tile(g, lambda g=g: weight_copy(g, True).wait_recv())
-
-                at = sum(spread(role, g, [weights[role, g]]) for g in range(3))
-                inv[...] += at.reshape(inv.shape)
-
-            each_role(spread_weights)
-
         force[...] = jnp.zeros(force.shape, jnp.float32)
 
         def spread_pulls(role, step=step):
             for batch in ((1,), (0, 2)):
+                if step == 0:
+
+                    @pl.when(role == 1)
+                    def _(batch=batch):
+                        for g in batch:
+                            when_tile(g, lambda g=g: weight_copy(g, True).wait_recv())
+
                 for g in batch:
                     when_tile(g, lambda g=g: value_copy(step, role, g, True).wait_recv())
                 at = 0.0
                 for g in batch:
-                    pull = weights[role, g] * (theirs[step, role, g] - mine[step, role, g])
-                    at = at + spread(role, g, [pull[0:1], pull[1:2]])
-                force[...] += at.reshape(force.shape)
+                    weight = weights[role, g]
+                    pull = weight * (theirs[step, role, g] - mine[step, role, g])
+                    values = [pull[0:1], pull[1:2]] + ([weight] if step == 0 else [])
+                    at = at + spread(role, g, values)
+                force[...] += at[: 2 * nodes_hi].reshape(force.shape)
+                if step == 0:
+                    inv[...] += at[2 * nodes_hi :].reshape(inv.shape)
 
         each_role(spread_pulls)
 

time: 12.7 us -> 12.7 us (level)
  no operation moved by 1% of the time
where the time goes in v4:
time: 12.7 us; the launch traced here: 12.6 us
  Pallas kernels  11.9 us (94%)
  local copies, waits for them, and re-layouts  0.63 us (5%)
    pallas_call x1, Pallas kernels, relax(): pl.pallas_call(functools.partial(kernel, n_sec, n_tile), out_shape=jax.Sh...  11.9 us
    unnamed x1, local copies, waits for them, and re-layouts  0.63 us

profile of v4, /device:TPU:0, one launch (start us, length us, event | category | flops | bytes accessed | tf_op | source)
XLA Modules:
  0.0 12.6 jit_solution(17073280906669897913)
XLA Ops:
  0.0 11.9 %shard_map.91 = f32[2,64,128]{2,1,0:T(8,128)S(1)} custom-call(f32[2,64,128]{2,1,0:T(8,128)} %bitcast.24, f32[64,128]{1,0:T(8,128)} %bitcast.25, f32[3,1,512]{2,1,0:T(1,128)} %bitcast.27, f32[3,2,512]{2,1,0:T(2,128)} %bitcast.26, s32[3,1,512]{2,1,0:T(1,128)} %bitcast.28, s32[3,1,512]{2,1,0:T(1,128)} %bitcast.29, s32[3,1,512]{2,1,0:T(1,128)} %bitcast.30, ...), custom_call_target="tpu_custom_call" | custom-call | tf_op jit(solution)/shard_map/pallas_call | solution.py:350
  12.0 0.6 %copy.14 = f32[1,2,2,4096]{3,2,1,0:T(2,128)} copy(f32[1,2,2,4096]{3,2,1,0:T(2,128)S(1)} %bitcast.23) | data formatting | bytes 131072

commit v5 on v4

--- a/solution.py
+++ b/solution.py
@@ -197,21 +197,29 @@
 
     each_role(prepare)
 
-    def pick(step, role):
+    def pick(step, comps, role):
+        start, count = comps[0] * nodes_hi, len(comps) * nodes_hi
         for g in (0, 2, 1):
             found = jnp.dot(
-                lhs[...],
+                lhs[pl.ds(start, count)],
                 hot_lo[role, :, pl.ds(g * slots, slots)],
                 preferred_element_type=jnp.float32,
             )
             hit = hi_node == hi_ids[role, g]
-            for k in range(2):
+            for i, k in enumerate(comps):
                 value = jnp.sum(
-                    jnp.where(hit, found[k * nodes_hi : (k + 1) * nodes_hi], 0.0),
+                    jnp.where(hit, found[i * nodes_hi : (i + 1) * nodes_hi], 0.0),
                     axis=0,
                     keepdims=True,
                 )
                 mine[step, role, g, pl.ds(k, 1), :] = value - off[role, g, pl.ds(k, 1), :]
+
+    def pick_all(step, comps):
+        for k in comps:
+            high, low = two_parts(field[k].reshape(nodes_hi, LANES))
+            lhs[pl.ds(k * nodes_hi, nodes_hi), pl.ds(0, LANES)] = high
+            lhs[pl.ds(k * nodes_hi, nodes_hi), pl.ds(LANES, LANES)] = low
+        each_role(functools.partial(pick, step, comps))
 
     def send_values(step, role):
         for g in (0, 2, 1):
@@ -251,11 +259,8 @@
                     edge_copy(step, side, k).wait_send()
 
     for step in range(STEPS):
-        for k in range(2):
-            part = two_parts(field[k].reshape(nodes_hi, LANES))
-            lhs[pl.ds(k * nodes_hi, nodes_hi), pl.ds(0, LANES)] = part[0]
-            lhs[pl.ds(k * nodes_hi, nodes_hi), pl.ds(LANES, LANES)] = part[1]
-        each_role(functools.partial(pick, step))
+        if step == 0:
+            pick_all(0, (0, 1))
         if step == 0:
             pl.semaphore_wait(barrier, greetings)
         each_role(functools.partial(send_values, step))
@@ -322,8 +327,10 @@
                     edge[step + 1, r, k] = c_row * new
                 else:
                     out[k, pl.ds(r, chunks, stride=2), :] = new
-            if step < STEPS - 1 and k == 0:
-                send_edges(step + 1, 0)
+            if step < STEPS - 1:
+                if k == 0:
+                    send_edges(step + 1, 0)
+                pick_all(step + 1, (k,))
 
     drain(STEPS - 1)
 

time: 12.7 us -> 12.8 us (level)
  no operation moved by 1% of the time
where the time goes in v5:
time: 12.8 us; the launch traced here: 12.7 us
  Pallas kernels  12 us (94%)
  local copies, waits for them, and re-layouts  0.63 us (5%)
    pallas_call x1, Pallas kernels, relax(): pl.pallas_call(functools.partial(kernel, n_sec, n_tile), out_shape=jax.Sh...  12 us
    unnamed x1, local copies, waits for them, and re-layouts  0.63 us

profile of v5, /device:TPU:0, one launch (start us, length us, event | category | flops | bytes accessed | tf_op | source)
XLA Modules:
  0.0 12.7 jit_solution(17916347659895753300)
XLA Ops:
  0.0 12.0 %shard_map.91 = f32[2,64,128]{2,1,0:T(8,128)S(1)} custom-call(f32[2,64,128]{2,1,0:T(8,128)} %bitcast.24, f32[64,128]{1,0:T(8,128)} %bitcast.25, f32[3,1,512]{2,1,0:T(1,128)} %bitcast.27, f32[3,2,512]{2,1,0:T(2,128)} %bitcast.26, s32[3,1,512]{2,1,0:T(1,128)} %bitcast.28, s32[3,1,512]{2,1,0:T(1,128)} %bitcast.29, s32[3,1,512]{2,1,0:T(1,128)} %bitcast.30, ...), custom_call_target="tpu_custom_call" | custom-call | tf_op jit(solution)/shard_map/pallas_call | solution.py:357
  12.1 0.6 %copy.14 = f32[1,2,2,4096]{3,2,1,0:T(2,128)} copy(f32[1,2,2,4096]{3,2,1,0:T(2,128)S(1)} %bitcast.23) | data formatting | bytes 131072

commit v6 on v4

--- a/solution.py
+++ b/solution.py
@@ -31,17 +31,11 @@
     return sums
 
 
-def two_parts(values):
-    high = values.astype(jnp.bfloat16)
-    low = (values - high.astype(jnp.float32)).astype(jnp.bfloat16)
-    return high, low
-
-
 def kernel(
     n_sec, n_tile, disp_in, stiff_in, wgt_in, off_in, srow_in, scol_in, trow_in, tcol_in, cnt_in,
     out,
     disp, stiff, wgt, off, rows, cols, cnt, load_sem,
-    field, force, total, inv, lhs, hot_lo, hot_hi, hi_ids, edge, halo, mine, theirs, weights,
+    field, force, total, inv, hot_lo, hot_hi, hi_ids, edge, halo, mine, theirs, weights,
     edge_send, edge_recv, val_send, val_recv, wgt_send, wgt_recv,
 ):
     sec = lax.axis_index("sec")
@@ -191,25 +185,28 @@
             hi_ids[role, g] = hi
             at = pl.ds(g * slots, slots)
             hot = jnp.where(lo_node == (col & (LANES - 1)), 1.0, 0.0).astype(jnp.bfloat16)
-            hot_lo[role, pl.ds(0, LANES), at] = hot
-            hot_lo[role, pl.ds(LANES, LANES), at] = hot
+            hot_lo[role, :, at] = hot
             hot_hi[role, :, at] = jnp.where(hi_node == hi, 1.0, 0.0).astype(jnp.bfloat16)
 
     each_role(prepare)
 
     def pick(step, role):
+        fields = [field[k].reshape(nodes_hi, LANES) for k in range(2)]
         for g in (0, 2, 1):
-            found = jnp.dot(
-                lhs[...],
-                hot_lo[role, :, pl.ds(g * slots, slots)],
-                preferred_element_type=jnp.float32,
-            )
+            lo = cols[role, g] & (LANES - 1)
             hit = hi_node == hi_ids[role, g]
             for k in range(2):
+                found = [
+                    jnp.take_along_axis(
+                        fields[k],
+                        jnp.broadcast_to(lo[:, at : at + LANES], (nodes_hi, LANES)),
+                        axis=1,
+                        mode="promise_in_bounds",
+                    )
+                    for at in range(0, slots, LANES)
+                ]
                 value = jnp.sum(
-                    jnp.where(hit, found[k * nodes_hi : (k + 1) * nodes_hi], 0.0),
-                    axis=0,
-                    keepdims=True,
+                    jnp.where(hit, jnp.concatenate(found, axis=1), 0.0), axis=0, keepdims=True
                 )
                 mine[step, role, g, pl.ds(k, 1), :] = value - off[role, g, pl.ds(k, 1), :]
 
@@ -223,7 +220,7 @@
         low = [(row - h.astype(jnp.float32)).astype(jnp.bfloat16) for row, h in zip(values, high)]
         summed = lax.dot_general(
             jnp.concatenate([hot_hi[role, :, at] * part for part in high + low], axis=0),
-            hot_lo[role, pl.ds(0, LANES), at],
+            hot_lo[role, :, at],
             (((1,), (1,)), ((), ())),
             preferred_element_type=jnp.float32,
         )
@@ -251,10 +248,6 @@
                     edge_copy(step, side, k).wait_send()
 
     for step in range(STEPS):
-        for k in range(2):
-            part = two_parts(field[k].reshape(nodes_hi, LANES))
-            lhs[pl.ds(k * nodes_hi, nodes_hi), pl.ds(0, LANES)] = part[0]
-            lhs[pl.ds(k * nodes_hi, nodes_hi), pl.ds(LANES, LANES)] = part[1]
         each_role(functools.partial(pick, step))
         if step == 0:
             pl.semaphore_wait(barrier, greetings)
@@ -365,8 +358,7 @@
             pltpu.VMEM((2, rows, chunks, LANES), f32),
             pltpu.VMEM((rows, chunks, LANES), f32),
             pltpu.VMEM((rows, chunks, LANES), f32),
-            pltpu.VMEM((2 * nodes_hi, 2 * LANES), jnp.bfloat16),
-            pltpu.VMEM((2, 2 * LANES, 3 * slots), jnp.bfloat16),
+            pltpu.VMEM((2, LANES, 3 * slots), jnp.bfloat16),
             pltpu.VMEM((2, nodes_hi, 3 * slots), jnp.bfloat16),
             pltpu.VMEM((2, 3, 1, slots), jnp.int32),
             pltpu.VMEM((STEPS, 2, 3, chunks, LANES), f32),

time: 12.7 us -> 12.8 us (level)
  no operation moved by 1% of the time
where the time goes in v6:
time: 12.8 us; the launch traced here: 12.7 us
  Pallas kernels  12 us (94%)
  local copies, waits for them, and re-layouts  0.63 us (5%)
    pallas_call x1, Pallas kernels, relax(): pl.pallas_call(functools.partial(kernel, n_sec, n_tile), out_shape=jax.Sh...  12 us
    unnamed x1, local copies, waits for them, and re-layouts  0.63 us

profile of v6, /device:TPU:0, one launch (start us, length us, event | category | flops | bytes accessed | tf_op | source)
XLA Modules:
  0.0 12.7 jit_solution(4388146325611550238)
XLA Ops:
  0.0 12.0 %shard_map.91 = f32[2,64,128]{2,1,0:T(8,128)S(1)} custom-call(f32[2,64,128]{2,1,0:T(8,128)} %bitcast.24, f32[64,128]{1,0:T(8,128)} %bitcast.25, f32[3,1,512]{2,1,0:T(1,128)} %bitcast.27, f32[3,2,512]{2,1,0:T(2,128)} %bitcast.26, s32[3,1,512]{2,1,0:T(1,128)} %bitcast.28, s32[3,1,512]{2,1,0:T(1,128)} %bitcast.29, s32[3,1,512]{2,1,0:T(1,128)} %bitcast.30, ...), custom_call_target="tpu_custom_call" | custom-call | tf_op jit(solution)/shard_map/pallas_call | solution.py:343
  12.0 0.6 %copy.14 = f32[1,2,2,4096]{3,2,1,0:T(2,128)} copy(f32[1,2,2,4096]{3,2,1,0:T(2,128)S(1)} %bitcast.23) | data formatting | bytes 131072

commit v7 on v4

--- a/solution.py
+++ b/solution.py
@@ -278,7 +278,7 @@
         force[...] = jnp.zeros(force.shape, jnp.float32)
 
         def spread_pulls(role, step=step):
-            for batch in ((1,), (0, 2)):
+            for batch in ((1, 0, 2),):
                 if step == 0:
 
                     @pl.when(role == 1)

time: 12.7 us -> 12.7 us (level)
  no operation moved by 1% of the time
where the time goes in v7:
time: 12.7 us; the launch traced here: 12.6 us
  Pallas kernels  11.9 us (94%)
  local copies, waits for them, and re-layouts  0.63 us (5%)
    pallas_call x1, Pallas kernels, relax(): pl.pallas_call(functools.partial(kernel, n_sec, n_tile), out_shape=jax.Sh...  11.9 us
    unnamed x1, local copies, waits for them, and re-layouts  0.63 us

profile of v7, /device:TPU:0, one launch (start us, length us, event | category | flops | bytes accessed | tf_op | source)
XLA Modules:
  0.0 12.6 jit_solution(14989939908709808509)
XLA Ops:
  0.0 11.9 %shard_map.91 = f32[2,64,128]{2,1,0:T(8,128)S(1)} custom-call(f32[2,64,128]{2,1,0:T(8,128)} %bitcast.24, f32[64,128]{1,0:T(8,128)} %bitcast.25, f32[3,1,512]{2,1,0:T(1,128)} %bitcast.27, f32[3,2,512]{2,1,0:T(2,128)} %bitcast.26, s32[3,1,512]{2,1,0:T(1,128)} %bitcast.28, s32[3,1,512]{2,1,0:T(1,128)} %bitcast.29, s32[3,1,512]{2,1,0:T(1,128)} %bitcast.30, ...), custom_call_target="tpu_custom_call" | custom-call | tf_op jit(solution)/shard_map/pallas_call | solution.py:350
  12.0 0.6 %copy.14 = f32[1,2,2,4096]{3,2,1,0:T(2,128)} copy(f32[1,2,2,4096]{3,2,1,0:T(2,128)S(1)} %bitcast.23) | data formatting | bytes 131072
